TPU v7x, 1024 devices: a whole 8x8x8 slice. The times are simulated.
1024 devices in a mesh: dp: 16 (over x, core), expert: 64 (over y, z).
Axes of the slice: x: 8, y: 8, z: 8, core: 2. Of those that a mesh axis runs over, the one named last changes fastest.
Arguments:
- tokens: bfloat16 [12288, 3584], P('expert'), may hold values from -6 to 6
- routes: int32 [12288, 2], P('expert'), may hold values from 0 to 63, all different within a row
- gates: float32 [12288, 2], P('expert'), may hold values from 0.1 to 0.9
- clusters: int32 [12288, 2], P('expert'), may hold values from 0 to 15
- counts: int32 [64, 64], P('expert'), may hold values from 1 to 2
- w_in: bfloat16 [64, 3584, 2432], P('expert', None, 'dp'), may hold values from -0.09375 to 0.09375
- w_out: bfloat16 [64, 2432, 3584], P('expert', 'dp'), may hold values from -0.125 to 0.125
- cotangent: bfloat16 [12288, 3584], P('expert'), may hold values from -6 to 6
Outputs:
- mixed: bfloat16 [12288, 3584], P('expert', 'dp')
- grad_tokens: bfloat16 [12288, 3584], P('expert', 'dp')
- grad_w_in: bfloat16 [64, 3584, 2432], P('expert', None, 'dp')
Inputs may be any that keep to these rules, and one draw needn't show every extreme that they name: `routes`: each token names two different experts, and every expert is named by some token.
All inputs are finite; a program needn't handle non-finite values.
Results may differ from a plain program's by a relative error of at most 0.0064.
Values may be sent and summed in bfloat16 or wider, within the bound.
A program may use at most 32 MiB of HBM per device.

v0:
```python
import jax
import jax.numpy as jnp
from jax import lax
from jax.sharding import PartitionSpec as P

SLOTS = 2


precise = lax.Precision.HIGHEST


def on_device(tokens, routes, gates, clusters, counts, w_in, w_out, cotangent):
    experts = counts.shape[1]
    slot_width = experts * SLOTS
    feature_total = tokens.shape[1]
    feature_count = feature_total // lax.axis_size("dp")
    feature_start = lax.axis_index("dp") * feature_count
    expert_ids = jnp.arange(experts, dtype=jnp.int32)
    live_count = jnp.sum(
        jnp.where(routes[:, :, None] == expert_ids[None, None, :], counts[0][None, None, :], 0),
        axis=2,
    )
    slot_ids = routes * SLOTS + jnp.remainder(clusters, live_count)
    slot_lanes = jnp.arange(slot_width, dtype=jnp.int32)
    picked = (slot_ids[:, :, None] == slot_lanes[None, None, :]).astype(jnp.float32)
    either = jnp.sum(picked, axis=1)
    weighted = jnp.sum(picked * gates[:, :, None], axis=1)
    member = jnp.maximum(jnp.sum(either, axis=0), 1.0)
    pooled_sum = lax.dot_general(
        either.astype(jnp.bfloat16),
        tokens,
        (((0,), (0,)), ((), ())),
        preferred_element_type=jnp.float32,
    )
    centre = (pooled_sum / member[:, None]).astype(jnp.bfloat16)
    back = lax.dot_general(
        weighted, cotangent.astype(jnp.float32), (((0,), (0,)), ((), ())), precision=precise
    )
    centre_recv, back_recv = (
        lax.all_to_all(
            centre.reshape(experts, SLOTS, feature_total),
            "expert",
            split_axis=0,
            concat_axis=0,
            tiled=True,
        ),
        lax.all_to_all(
            back.astype(jnp.bfloat16).reshape(experts, SLOTS, feature_total),
            "expert",
            split_axis=0,
            concat_axis=0,
            tiled=True,
        ),
    )
    centre_rows = centre_recv.reshape(-1, feature_total)
    back_rows = back_recv.reshape(-1, feature_total)
    centre_slice = lax.dynamic_slice_in_dim(centre, feature_start, feature_count, 1)
    back_slice = lax.dynamic_slice_in_dim(back, feature_start, feature_count, 1)
    row_total = centre_rows.shape[0]
    weight_in = w_in[0]
    weight_out = w_out[0]
    preact = jnp.dot(centre_rows, weight_in, preferred_element_type=jnp.float32)
    hidden_grad = lax.dot_general(
        back_rows, weight_out, (((1,), (1,)), ((), ())), preferred_element_type=jnp.float32
    )
    hidden = jax.nn.silu(preact).astype(jnp.bfloat16)
    sigmoid_val = jax.nn.sigmoid(preact)
    preact_grad = (hidden_grad * sigmoid_val * (1.0 + preact * (1.0 - sigmoid_val))).astype(
        jnp.bfloat16
    )
    out_part = lax.dot_general(
        weight_out, hidden, (((0,), (1,)), ((), ())), preferred_element_type=jnp.float32
    )
    grad_part = lax.dot_general(
        weight_in, preact_grad, (((1,), (1,)), ((), ())), preferred_element_type=jnp.float32
    )
    shared = lax.psum_scatter(
        jnp.concatenate([out_part, grad_part], axis=1).astype(jnp.bfloat16),
        "dp",
        scatter_dimension=0,
        tiled=True,
    )
    expert_part, centre_part = (
        lax.all_to_all(shared[:, :row_total], "expert", split_axis=1, concat_axis=1, tiled=True),
        lax.all_to_all(shared[:, row_total:], "expert", split_axis=1, concat_axis=1, tiled=True),
    )
    weight_grad = lax.dot_general(
        centre_rows, preact_grad, (((0,), (0,)), ((), ())), preferred_element_type=jnp.float32
    ).astype(jnp.bfloat16)
    token_slice = lax.dynamic_slice_in_dim(tokens, feature_start, feature_count, 1)
    cotangent_slice = lax.dynamic_slice_in_dim(cotangent, feature_start, feature_count, 1)
    gate_sum = 1.0 + jnp.sum(gates, axis=1)
    carried = expert_part.T.astype(jnp.float32) - centre_slice.astype(jnp.float32)
    mixed = token_slice.astype(jnp.float32) * gate_sum[:, None] + jnp.dot(
        weighted, carried, precision=precise
    )
    pulled = (centre_part.T.astype(jnp.float32) - back_slice) / member[:, None]
    grad_tokens = cotangent_slice.astype(jnp.float32) * gate_sum[:, None] + jnp.dot(
        either, pulled, precision=precise
    )
    return (mixed.astype(jnp.bfloat16), grad_tokens.astype(jnp.bfloat16), weight_grad[None])


def solution(mesh):
    in_specs = (
        P("expert", None),
        P("expert", None),
        P("expert", None),
        P("expert", None),
        P("expert", None),
        P("expert", None, "dp"),
        P("expert", "dp", None),
        P("expert", None),
    )
    out_specs = (P("expert", "dp"), P("expert", "dp"), P("expert", None, "dp"))
    return jax.shard_map(
        on_device, mesh=mesh, in_specs=in_specs, out_specs=out_specs, check_vma=False
    )
```

profile of v0, /device:TPU:16, one launch (start us, length us, event | category | flops | bytes accessed | tf_op | source)
XLA Modules:
  0.0 218.1 jit_solution(8842115444991173930)
XLA Ops:
  7.2 0.0 copy-start
  7.2 0.9 select_reduce_fusion.1
  8.1 0.8 fusion.21
  8.9 0.9 convert_reduce_fusion.1
  9.8 1.8 fusion
  11.6 0.0 copy-start.4
  11.6 1.3 reshape.36
  12.8 0.0 copy-done.4
  12.8 23.3 %all-to-all-start = ((bf16[64,2,3584]{2,1,0:T(2,128)(2,1)}), bf16[64,2,3584]{2,1,0:T(2,128)(2,1)S(1)}, u32[]{:S(2)}, u32[]{:S(2)}) async-start(bf16[64,2,3584]{2,1,0:T(2,128)(2,1)} %reshape.36), calls=%async_computation | async-start | bytes 1835008 | tf_op jit(solution)/shard_map/all_to_all | solution.py:40
  36.2 3.5 %fusion.26 = (bf16[128,3584]{1,0:T(8,128)(2,1)S(1)}, f32[128,3584]{1,0:T(8,128)}) fusion(f32[192,128]{1,0:T(8,128)S(1)} %get-tuple-element.5, bf16[192,3584]{1,0:T(8,128)(2,1)} %param.15), kind=kOutput, calls=%fused_computation.47 | convolution fusion | flops 1057423360 | bytes 4227072 | tf_op jit(solution)/shard_map/dot_general | solution.py:36
  39.7 1.3 reshape.38
  40.9 21.9 %all-to-all-done = bf16[64,2,3584]{2,1,0:T(2,128)(2,1)S(1)} async-done(((bf16[64,2,3584]{2,1,0:T(2,128)(2,1)}), bf16[64,2,3584]{2,1,0:T(2,128)(2,1)S(1)}, u32[]{:S(2)}, u32[]{:S(2)}) %all-to-all-start) | async-done | bytes 917536 | tf_op jit(solution)/shard_map/all_to_all | solution.py:40
  62.8 0.0 copy-start.2
  62.8 6.7 %all-to-all-start.1 = ((bf16[64,2,3584]{2,1,0:T(2,128)(2,1)}), bf16[64,2,3584]{2,1,0:T(2,128)(2,1)}, u32[]{:S(2)}, u32[]{:S(2)}) async-start(bf16[64,2,3584]{2,1,0:T(2,128)(2,1)} %reshape.38), calls=%async_computation.1 | async-start | bytes 1835008 | tf_op jit(solution)/shard_map/all_to_all | solution.py:47
  69.5 0.0 copy-done.2
  69.5 0.0 copy-start.1
  69.5 0.0 reduce-scatter.4.cloned.1.call-start
  69.5 2.6 %reshape.37 = bf16[128,3584]{1,0:T(8,128)(2,1)S(1)} reshape(bf16[64,2,3584]{2,1,0:T(2,128)(2,1)} %copy-done.2) | data formatting | bytes 1835008 | tf_op jit(solution)/shard_map/reshape | solution.py:55
  72.1 0.0 copy-done.1
  72.1 0.4 fusion.11
  72.6 0.0 copy-done
  72.6 1.4 fusion.2
  74.0 21.7 %all-to-all-done.1 = bf16[64,2,3584]{2,1,0:T(2,128)(2,1)} async-done(((bf16[64,2,3584]{2,1,0:T(2,128)(2,1)}), bf16[64,2,3584]{2,1,0:T(2,128)(2,1)}, u32[]{:S(2)}, u32[]{:S(2)}) %all-to-all-start.1) | async-done | bytes 917536 | tf_op jit(solution)/shard_map/all_to_all | solution.py:47
  95.6 3.2 %reshape.39 = bf16[128,3584]{1,0:T(8,128)(2,1)} reshape(bf16[64,2,3584]{2,1,0:T(2,128)(2,1)} %all-to-all-done.1) | data formatting | bytes 1835008 | tf_op jit(solution)/shard_map/reshape | solution.py:56
  98.8 1.6 fusion.7
  100.5 0.0 copy-start.3
  100.5 0.4 fusion.3
  100.9 0.7 copy-done.3
  101.6 1.4 pad_maximum_fusion
  103.0 3.8 %copy.20 = bf16[3584,256]{1,0:T(8,128)(2,1)} copy(bf16[3584,256]{0,1:T(8,128)(2,1)} %pad_maximum_fusion) | data formatting | bytes 3670016
  106.8 0.0 copy-start.5
  106.8 0.0 reduce-scatter.4.cloned.1.call-update
  106.8 0.6 copy-done.5
  107.5 57.7 %reduce-scatter.4.cloned.1.call-done = bf16[224,256]{1,0:T(8,128)(2,1)} async-done(((bf16[3584,256]{1,0:T(8,128)(2,1)}), bf16[224,256]{1,0:T(8,128)(2,1)}) %reduce-scatter.4.cloned.1.call-update) | async-done | bytes 114704
  165.2 0.9 fusion.25
  166.1 0.1 copy.22
  166.2 0.7 all_to_all.20
  166.9 14.0 %all-to-all-start.2 = ((bf16[224,64,2]{0,2,1:T(2,128)(2,1)}), bf16[224,64,2]{0,2,1:T(2,128)(2,1)S(1)}, u32[]{:S(2)}, u32[]{:S(2)}) async-start(bf16[224,64,2]{0,2,1:T(2,128)(2,1)} %all_to_all.20), calls=%async_computation.2 | async-start | bytes 131072 | tf_op jit(solution)/shard_map/all_to_all | solution.py:84
  180.9 1.4 fusion.1
  182.3 0.1 copy.23
  182.4 0.7 all_to_all.22
  183.1 9.2 %all-to-all-done.2 = bf16[224,64,2]{0,2,1:T(2,128)(2,1)S(1)} async-done(((bf16[224,64,2]{0,2,1:T(2,128)(2,1)}), bf16[224,64,2]{0,2,1:T(2,128)(2,1)S(1)}, u32[]{:S(2)}, u32[]{:S(2)}) %all-to-all-start.2) | async-done | bytes 57376 | tf_op jit(solution)/shard_map/all_to_all | solution.py:84
  192.3 5.4 %all-to-all-start.3 = ((bf16[224,64,2]{0,2,1:T(2,128)(2,1)}), bf16[224,64,2]{0,2,1:T(2,128)(2,1)S(1)}, u32[]{:S(2)}, u32[]{:S(2)}) async-start(bf16[224,64,2]{0,2,1:T(2,128)(2,1)} %all_to_all.22), calls=%async_computation.3 | async-start | bytes 131072 | tf_op jit(solution)/shard_map/all_to_all | solution.py:85
  197.7 0.1 reshape.40
  197.8 2.0 fusion.4
  199.8 9.4 %all-to-all-done.3 = bf16[224,64,2]{0,2,1:T(2,128)(2,1)S(1)} async-done(((bf16[224,64,2]{0,2,1:T(2,128)(2,1)}), bf16[224,64,2]{0,2,1:T(2,128)(2,1)S(1)}, u32[]{:S(2)}, u32[]{:S(2)}) %all-to-all-start.3) | async-done | bytes 57376 | tf_op jit(solution)/shard_map/all_to_all | solution.py:85
  209.1 0.1 reshape.41
  209.2 2.1 fusion.5
  (3 shorter events, 0.0 us)
Async XLA Ops:
  7.2 65.4 %copy-start = (bf16[1,152,3584]{2,1,0:T(8,128)(2,1)S(1)}, bf16[1,152,3584]{2,1,0:T(8,128)(2,1)}, u32[]{:S(2)}) copy-start(bf16[1,152,3584]{2,1,0:T(8,128)(2,1)} %param.14) | copy-start | bytes 3268612
  11.6 1.3 copy-start.4
  12.8 50.0 %all-to-all-start = ((bf16[64,2,3584]{2,1,0:T(2,128)(2,1)}), bf16[64,2,3584]{2,1,0:T(2,128)(2,1)S(1)}, u32[]{:S(2)}, u32[]{:S(2)}) async-start(bf16[64,2,3584]{2,1,0:T(2,128)(2,1)} %reshape.36), calls=%async_computation | async-start | bytes 1835008 | tf_op jit(solution)/shard_map/all_to_all | solution.py:40
  62.8 6.7 %copy-start.2 = (bf16[64,2,3584]{2,1,0:T(2,128)(2,1)}, bf16[64,2,3584]{2,1,0:T(2,128)(2,1)S(1)}, u32[]{:S(2)}) copy-start(bf16[64,2,3584]{2,1,0:T(2,128)(2,1)S(1)} %all-to-all-done) | copy-start | bytes 2752516
  62.8 32.8 %all-to-all-start.1 = ((bf16[64,2,3584]{2,1,0:T(2,128)(2,1)}), bf16[64,2,3584]{2,1,0:T(2,128)(2,1)}, u32[]{:S(2)}, u32[]{:S(2)}) async-start(bf16[64,2,3584]{2,1,0:T(2,128)(2,1)} %reshape.38), calls=%async_computation.1 | async-start | bytes 1835008 | tf_op jit(solution)/shard_map/all_to_all | solution.py:47
  69.5 2.6 %copy-start.1 = (bf16[1,3584,152]{1,2,0:T(8,128)(2,1)S(1)}, bf16[1,3584,152]{1,2,0:T(8,128)(2,1)}, u32[]{:S(2)}) copy-start(bf16[1,3584,152]{1,2,0:T(8,128)(2,1)} %param.13) | copy-start | bytes 3268612
  69.5 95.7 %reduce-scatter.4.cloned.1.call-start = ((), (), s32[]{:S(2)}) async-start(), calls=%async_computation.5 | async-start | bytes 1949696
  100.5 1.2 copy-start.3
  106.8 0.7 copy-start.5
  166.9 25.4 %all-to-all-start.2 = ((bf16[224,64,2]{0,2,1:T(2,128)(2,1)}), bf16[224,64,2]{0,2,1:T(2,128)(2,1)S(1)}, u32[]{:S(2)}, u32[]{:S(2)}) async-start(bf16[224,64,2]{0,2,1:T(2,128)(2,1)} %all_to_all.20), calls=%async_computation.2 | async-start | bytes 131072 | tf_op jit(solution)/shard_map/all_to_all | solution.py:84
  192.3 16.9 %all-to-all-start.3 = ((bf16[224,64,2]{0,2,1:T(2,128)(2,1)}), bf16[224,64,2]{0,2,1:T(2,128)(2,1)S(1)}, u32[]{:S(2)}, u32[]{:S(2)}) async-start(bf16[224,64,2]{0,2,1:T(2,128)(2,1)} %all_to_all.22), calls=%async_computation.3 | async-start | bytes 131072 | tf_op jit(solution)/shard_map/all_to_all | solution.py:85
Sparse Core Ops, SparseCore 0:
  106.9 58.2 reduce-scatter.3
where the time goes:
time: 219 us; the launch traced here: 218 us
  waiting for transfers between devices  120 us (55%)
  starting transfers between devices  49.4 us (23%)
  local copies, waits for them, and re-layouts  16 us (7%)
  matrix products  14.7 us (7%)
  between operations  14.2 us (6%)
  other arithmetic  3.97 us (2%)
    unnamed x2, waiting for transfers between devices  57.7 us
    all_to_all x1, starting transfers between devices, on_device(): lax.all_to_all(centre.reshape(experts, SLOTS, feature_total), 'expert', s...  23.3 us
    all_to_all x1, waiting for transfers between devices, on_device(): lax.all_to_all(centre.reshape(experts, SLOTS, feature_total), 'expert', s...  21.9 us
    all_to_all x1, waiting for transfers between devices, on_device(): lax.all_to_all(back.astype(jnp.bfloat16).reshape(experts, SLOTS, feature_...  21.7 us
    all_to_all x1, starting transfers between devices, on_device(): lax.all_to_all(shared[:, :row_total], 'expert', split_axis=1, concat_axis...  14 us
    all_to_all x1, waiting for transfers between devices, on_device(): lax.all_to_all(shared[:, row_total:], 'expert', split_axis=1, concat_axis...  9.38 us
    all_to_all x1, waiting for transfers between devices, on_device(): lax.all_to_all(shared[:, :row_total], 'expert', split_axis=1, concat_axis...  9.18 us
    all_to_all x1, starting transfers between devices, on_device(): lax.all_to_all(back.astype(jnp.bfloat16).reshape(experts, SLOTS, feature_...  6.65 us
  transfers between devices with their start and end apart: 5, of which 5 were waited for; matrix products, arithmetic and copies ran while one was open for 6% of the time, Pallas kernels for 0%

commit v1 on v0

v1 whole, which is shorter than its diff:
```python
import functools

import jax
import jax.numpy as jnp
from jax import lax
from jax.experimental import pallas as pl
from jax.experimental.pallas import tpu as pltpu
from jax.sharding import PartitionSpec as P

SLOTS = 2
LANES = 128
CHIPS = 8
MESH = pl.DeviceIdType.MESH
BF16 = jnp.bfloat16
F32 = jnp.float32
REACH = (4, 3, 5, 2, 6, 1, 7, 0)


def nn(a, b):
    return lax.dot_general(a, b, (((1,), (0,)), ((), ())), preferred_element_type=F32)


def nt(a, b):
    return lax.dot_general(a, b, (((1,), (1,)), ((), ())), preferred_element_type=F32)


def split(value):
    high = value.astype(BF16)
    return high, (value - high.astype(F32)).astype(BF16)


def eye(size):
    rows = lax.broadcasted_iota(jnp.int32, (size, size), 0)
    return (rows == lax.broadcasted_iota(jnp.int32, (size, size), 1)).astype(BF16)


def kernel(
    shape,
    tokens, routes, gates, clusters, counts, w_in, w_out, cotangent,
    mixed_out, grad_tokens_out, grad_w_out,
    tok_win, cot_win, routes_v, gates_v, clusters_v, counts_v, win_v, wout_v,
    win_t, wout_t, wout_q, perm, perm_t,
    either_t, weight_t, either_r, weight_r, gate_col, member_v, tok_s, cot_s, centre_v, back_v,
    send1, recv1, send2, recv2,
    gathered, pre_v, part, sib_out, sib_in, right_out, left_out, right_in, left_in, far_out, far_in,
    mixed_v, grad_v, gw_v,
    in_sem, hop_sem, ag_send, ag_recv, rs_send, rs_recv, out_sem,
):
    experts, toks, feats, units = shape
    slots = experts * SLOTS
    half = feats // 2
    upper = feats - LANES
    dp = lax.axis_index("dp")
    me = lax.axis_index("expert")
    chip = dp // 2
    core = lax.rem(dp, 2)
    right = lax.rem(chip + 1, CHIPS) * 2 + core
    left = lax.rem(chip + CHIPS - 1, CHIPS) * 2 + core
    sibling = chip * 2 + 1 - core

    def shard(distance, of_core):
        return lax.rem(chip + distance, CHIPS) * 2 + of_core

    width = tokens.shape[1]
    window = tok_win.shape[1]
    tile = jnp.minimum(dp * feats // LANES, (width - window) // LANES)
    start = pl.multiple_of(tile * LANES, LANES)
    shift = dp * feats - tile * LANES

    loads = [
        pltpu.make_async_copy(src, dst, in_sem.at[i])
        for i, (src, dst) in enumerate((
            (routes, routes_v), (clusters, clusters_v), (gates, gates_v), (counts, counts_v),
            (tokens.at[:, pl.ds(start, window)], tok_win),
            (cotangent.at[:, pl.ds(start, window)], cot_win),
            (w_out.at[0], wout_v), (w_in.at[0], win_v),
        ))
    ]
    for load in loads:
        load.start()

    barrier = pltpu.get_barrier_semaphore()

    @pl.loop(1, experts)
    def _(k):
        pl.semaphore_signal(
            barrier, inc=1, device_id=(dp, lax.rem(me + k, experts)), device_id_type=MESH
        )

    for there in (right, left, sibling):
        pl.semaphore_signal(barrier, inc=1, device_id=(there, me), device_id_type=MESH)

    rows = lax.broadcasted_iota(jnp.int32, (4 * slots, 4 * slots), 0)
    cols = lax.broadcasted_iota(jnp.int32, (4 * slots, 4 * slots), 1)
    perm[...] = (cols == ((rows % 8) // 2) * slots + (rows // 8) * 2 + rows % 2).astype(F32).astype(BF16)
    perm_t[...] = (rows == ((cols % 8) // 2) * slots + (cols // 8) * 2 + cols % 2).astype(F32).astype(BF16)

    for load in loads[:4]:
        load.wait()
    expert_rows = lax.broadcasted_iota(jnp.int32, (experts, experts), 0)
    expert_cols = lax.broadcasted_iota(jnp.int32, (experts, experts), 1)
    live_col = jnp.sum(jnp.where(expert_rows == expert_cols, counts_v[...], 0), axis=1, keepdims=True)
    ids = lax.broadcasted_iota(jnp.int32, (experts, toks), 0)
    slot_rows = lax.broadcasted_iota(jnp.int32, (slots, toks), 0)
    hits, weights = [], []
    for k in range(2):
        route = routes_v[k : k + 1, :]
        live = jnp.sum(jnp.where(ids == route, live_col, 0), axis=0, keepdims=True)
        slot = route * SLOTS + jnp.where(live == 2, clusters_v[k : k + 1, :] & 1, 0)
        hits.append((slot_rows == slot).astype(F32))
        weights.append(hits[-1] * gates_v[k : k + 1, :])
    either = hits[0] + hits[1]
    weight_hi, weight_lo = split(weights[0] + weights[1])
    member = jnp.maximum(jnp.sum(either, axis=1, keepdims=True), 1.0)
    member_v[...] = jnp.broadcast_to(member, member_v.shape)
    either_t[...] = either.astype(BF16)
    weight_t[0] = weight_hi
    weight_t[1] = weight_lo

    pick_rows = lax.broadcasted_iota(jnp.int32, (window, 2 * LANES), 0)
    pick_cols = lax.broadcasted_iota(jnp.int32, (window, 2 * LANES), 1)
    pick = ((pick_rows == pick_cols + shift) & (pick_cols < feats)).astype(F32).astype(BF16)
    loads[4].wait()
    tok_s[...] = nn(tok_win[...], pick).astype(BF16)
    centre_v[...] = (nn(either_t[...], tok_s[...]) / member_v[...]).astype(BF16)
    loads[5].wait()
    cot_s[...] = nn(cot_win[...], pick).astype(BF16)
    back = nn(weight_t[0], cot_s[...]) + nn(weight_t[1], cot_s[...])
    back_v[...] = back
    sent = back.astype(BF16)
    stacked = jnp.concatenate(
        [centre_v[:, :LANES], centre_v[:, LANES:], sent[:, :LANES], sent[:, LANES:]], axis=0
    )
    send1[...] = nn(perm[...], stacked).astype(BF16).reshape(experts, 8, LANES)

    def exchange(send, recv, sem):
        own = pltpu.make_async_copy(send.at[me], recv.at[me], hop_sem.at[sem])
        own.start()

        @pl.loop(1, experts)
        def _(k):
            peer = lax.rem(me + k, experts)
            pltpu.make_async_remote_copy(
                src_ref=send.at[peer], dst_ref=recv.at[me],
                send_sem=hop_sem.at[sem + 1], recv_sem=hop_sem.at[sem + 2],
                device_id=(dp, peer), device_id_type=MESH,
            ).start()

        return own

    def exchanged(own, send, recv, sem):
        own.wait()
        rest = pl.ds(0, experts - 1)
        pltpu.make_async_copy(recv.at[rest], recv.at[rest], hop_sem.at[sem + 2]).wait()

    def sent_all(send, sem):
        rest = pl.ds(0, experts - 1)
        pltpu.make_async_copy(send.at[rest], send.at[rest], hop_sem.at[sem + 1]).wait()

    pl.semaphore_wait(barrier, experts + 2)
    own1 = exchange(send1, recv1, 0)

    token_eye = eye(toks)
    either_r[...] = nt(token_eye, either_t[...]).astype(BF16)
    weight_r[0] = nt(token_eye, weight_t[0]).astype(BF16)
    weight_r[1] = nt(token_eye, weight_t[1]).astype(BF16)
    gate_row = 1.0 + jnp.sum(gates_v[...], axis=0, keepdims=True)
    gate_col[...] = jnp.broadcast_to(
        jnp.sum(jnp.where(token_eye.astype(F32) > 0.0, gate_row, 0.0), axis=1, keepdims=True), gate_col.shape
    )
    loads[6].wait()
    lane_eye = eye(LANES)

    @pl.loop(0, width // LANES)
    def _(j):
        at = pl.multiple_of(j * LANES, LANES)
        wout_t[pl.ds(at, LANES), :] = nt(lane_eye, wout_v[:, pl.ds(at, LANES)]).astype(BF16)

    loads[7].wait()
    unit_eye = eye(units)

    @pl.loop(0, 2 * CHIPS)
    def _(q):
        at = pl.ds(pl.multiple_of(q * feats, 32), feats)
        win_t[q] = nt(unit_eye, win_v[at, :]).astype(BF16)
        wout_q[q] = nt(unit_eye, wout_t[at, :]).astype(BF16)

    exchanged(own1, send1, recv1, 0)
    arrived = lax.dot_general(
        recv1[...].reshape(4 * slots, LANES), perm[...], (((0,), (0,)), ((), ())), preferred_element_type=F32
    ).astype(BF16)
    for kind in range(2):
        gathered[kind, dp, 0:LANES, :] = arrived[:, 2 * kind * slots : (2 * kind + 1) * slots]
        gathered[kind, dp, LANES:feats, :] = arrived[0:upper, (2 * kind + 1) * slots : (2 * kind + 2) * slots]

    pending = []

    def pass_on(kind, lane, which, rows, there):
        at = pl.ds(*rows)
        copy = pltpu.make_async_remote_copy(
            src_ref=gathered.at[kind, which, at], dst_ref=gathered.at[kind, which, at],
            send_sem=ag_send.at[kind, lane], recv_sem=ag_recv.at[kind, lane],
            device_id=(there, me), device_id_type=MESH,
        )
        copy.start()
        pending.append(copy)

    def landed(kind, lane, which, rows):
        at = pl.ds(*rows)
        pltpu.make_async_copy(gathered.at[kind, which, at], gathered.at[kind, which, at], ag_recv.at[kind, lane]).wait()

    whole, first, second = (0, feats), (0, half), (half, half)
    for kind in range(2):
        pass_on(kind, 0, dp, whole, right)
        pass_on(kind, 4, dp, whole, left)
        pass_on(kind, 8, dp, whole, sibling)

    forms = (win_t, wout_q)

    def contract(kind, which):
        pre_v[kind] += nn(forms[kind][which], gathered[kind, which])

    for kind in range(2):
        pre_v[kind] = nn(forms[kind][dp], gathered[kind, dp])

    def step(kind, hop):
        behind, ahead = shard(CHIPS - hop, core), shard(hop, core)
        from_left = first if hop == 4 else whole
        from_right = second if hop == 4 else whole
        landed(kind, hop - 1, behind, from_left)
        if hop < 4:
            pass_on(kind, hop, behind, first if hop == 3 else whole, right)
        pass_on(kind, 8 + hop, behind, from_left, sibling)
        landed(kind, 3 + hop, ahead, from_right)
        if hop < 4:
            pass_on(kind, 4 + hop, ahead, second if hop == 3 else whole, left)
        pass_on(kind, 12 + hop, ahead, from_right, sibling)

    def use(kind, hop):
        if hop == 0:
            landed(kind, 8, sibling, whole)
            contract(kind, sibling)
            return
        contract(kind, shard(CHIPS - hop, core))
        if hop < 4:
            contract(kind, shard(hop, core))
        other = 1 - core
        landed(kind, 8 + hop, shard(CHIPS - hop, other), first if hop == 4 else whole)
        landed(kind, 12 + hop, shard(hop, other), second if hop == 4 else whole)
        contract(kind, shard(CHIPS - hop, other))
        if hop < 4:
            contract(kind, shard(hop, other))

    for hop in range(1, 5):
        for kind in range(2):
            step(kind, hop)
        for kind in range(2):
            use(kind, hop - 1)
    for kind in range(2):
        use(kind, 4)

    preact = pre_v[0]
    sigmoid_val = jax.nn.sigmoid(preact)
    hidden = (preact * sigmoid_val).astype(BF16)
    preact_grad = (pre_v[1] * sigmoid_val * (1.0 + preact * (1.0 - sigmoid_val))).astype(BF16)

    summed = []
    for kind, (weights_of, units_of) in enumerate(((wout_t, hidden), (win_v, preact_grad))):
        for d in REACH:
            theirs = pl.ds(pl.multiple_of(shard(d, 1 - core) * feats, 32), feats)
            sib_out[kind, d] = nn(weights_of[theirs, :], units_of).astype(BF16)
            copy = pltpu.make_async_remote_copy(
                src_ref=sib_out.at[kind, d], dst_ref=sib_in.at[kind, d],
                send_sem=rs_send.at[kind, d], recv_sem=rs_recv.at[kind, d],
                device_id=(sibling, me), device_id_type=MESH,
            )
            copy.start()
            summed.append(copy)
            ours = pl.ds(pl.multiple_of(shard(d, core) * feats, 32), feats)
            part[kind, d] = nn(weights_of[ours, :], units_of)

    def both(kind, d):
        pltpu.make_async_copy(sib_in.at[kind, d], sib_in.at[kind, d], rs_recv.at[kind, d]).wait()
        return part[kind, d] + sib_in[kind, d].astype(F32)

    def push(kind, lane, out, into, there):
        copy = pltpu.make_async_remote_copy(
            src_ref=out, dst_ref=into,
            send_sem=rs_send.at[kind, lane], recv_sem=rs_recv.at[kind, lane],
            device_id=(there, me), device_id_type=MESH,
        )
        copy.start()
        summed.append(copy)

    def came(kind, lane, into):
        pltpu.make_async_copy(into, into, rs_recv.at[kind, lane]).wait()
        return into[...].astype(F32)

    def chain(kind, hop):
        if hop == 0:
            total = both(kind, 4)
            far_out[kind, 0] = total[:half].astype(BF16)
            far_out[kind, 1] = total[half:].astype(BF16)
            push(kind, 8, far_out.at[kind, 0], far_in.at[kind, 0], right)
            push(kind, 12, far_out.at[kind, 1], far_in.at[kind, 1], left)
            return
        to_right, to_left = both(kind, 4 - hop), both(kind, 4 + hop)
        if hop == 1:
            right_out[kind, 0, :half] = (to_right[:half] + came(kind, 8, far_in.at[kind, 0])).astype(BF16)
            right_out[kind, 0, half:] = to_right[half:].astype(BF16)
            left_out[kind, 0, :half] = to_left[:half].astype(BF16)
            left_out[kind, 0, half:] = (to_left[half:] + came(kind, 12, far_in.at[kind, 1])).astype(BF16)
        else:
            right_out[kind, hop - 1] = (to_right + came(kind, 7 + hop, right_in.at[kind, hop - 2])).astype(BF16)
            left_out[kind, hop - 1] = (to_left + came(kind, 11 + hop, left_in.at[kind, hop - 2])).astype(BF16)
        push(kind, 8 + hop, right_out.at[kind, hop - 1], right_in.at[kind, hop - 1], right)
        push(kind, 12 + hop, left_out.at[kind, hop - 1], left_in.at[kind, hop - 1], left)

    def weight_grads(low, high):
        @pl.loop(low, high)
        def _(q):
            at = pl.ds(pl.multiple_of(q * feats, 32), feats)
            gw_v[at, :] = nt(gathered[0, q], preact_grad).astype(BF16)

    for hop in range(4):
        for kind in range(2):
            chain(kind, hop)
        weight_grads(4 * hop, 4 * hop + 4)
    gw_copy = pltpu.make_async_copy(gw_v, grad_w_out.at[0], out_sem.at[0])
    gw_copy.start()

    pieces = []
    for kind in range(2):
        total = both(kind, 0)
        total += came(kind, 11, right_in.at[kind, 2]) + came(kind, 15, left_in.at[kind, 2])
        total = total.astype(BF16)
        pieces += [total[:LANES], jnp.concatenate([total[LANES:], jnp.zeros((LANES - upper, slots), BF16)], axis=0)]
    send2[...] = nt(perm[...], jnp.concatenate(pieces, axis=1)).astype(BF16).reshape(experts, 8, LANES)
    own2 = exchange(send2, recv2, 3)

    scaled_tok = [tok_s[:, i * LANES : (i + 1) * LANES].astype(F32) * gate_col[...] for i in range(2)]
    scaled_cot = [cot_s[:, i * LANES : (i + 1) * LANES].astype(F32) * gate_col[...] for i in range(2)]
    scale = 1.0 / member_v[:, :LANES]
    for copy in pending + summed:
        copy.wait_send()
    sent_all(send1, 0)

    exchanged(own2, send2, recv2, 3)
    ordered = nn(perm_t[...], recv2[...].reshape(4 * slots, LANES))
    for i, (low, count) in enumerate(((0, LANES), (LANES, upper))):
        carried = ordered[i * slots : (i + 1) * slots] - centre_v[:, i * LANES : (i + 1) * LANES].astype(F32)
        pulled = (ordered[(2 + i) * slots : (3 + i) * slots] - back_v[:, i * LANES : (i + 1) * LANES]) * scale
        high, rest = split(carried)
        mixed = scaled_tok[i] + nn(weight_r[0], high) + nn(weight_r[0], rest) + nn(weight_r[1], high)
        mixed_v[:, low : low + count] = mixed[:, :count].astype(BF16)
        high, rest = split(pulled)
        grads = scaled_cot[i] + nn(either_r[...], high) + nn(either_r[...], rest)
        grad_v[:, low : low + count] = grads[:, :count].astype(BF16)
    mixed_copy = pltpu.make_async_copy(mixed_v, mixed_out, out_sem.at[1])
    mixed_copy.start()
    grad_copy = pltpu.make_async_copy(grad_v, grad_tokens_out, out_sem.at[2])
    grad_copy.start()
    sent_all(send2, 3)
    gw_copy.wait()
    mixed_copy.wait()
    grad_copy.wait()


def on_device(tokens, routes, gates, clusters, counts, w_in, w_out, cotangent):
    toks, width = tokens.shape
    experts = counts.shape[1]
    shards = lax.axis_size("dp")
    units = w_in.shape[2]
    feats = width // shards
    slots = experts * SLOTS
    vmem = pltpu.VMEM
    dma = pltpu.SemaphoreType.DMA
    scratch = [
        vmem((toks, 3 * LANES), BF16), vmem((toks, 3 * LANES), BF16),
        vmem((2, toks), jnp.int32), vmem((2, toks), F32), vmem((2, toks), jnp.int32), vmem((1, experts), jnp.int32),
        vmem((width, units), BF16), vmem((units, width), BF16),
        vmem((shards, units, feats), BF16), vmem((width, units), BF16), vmem((shards, units, feats), BF16),
        vmem((4 * slots, 4 * slots), BF16), vmem((4 * slots, 4 * slots), BF16),
        vmem((slots, toks), BF16), vmem((2, slots, toks), BF16),
        vmem((toks, slots), BF16), vmem((2, toks, slots), BF16),
        vmem((toks, LANES), F32), vmem((slots, 2 * LANES), F32),
        vmem((toks, 2 * LANES), BF16), vmem((toks, 2 * LANES), BF16),
        vmem((slots, 2 * LANES), BF16), vmem((slots, 2 * LANES), F32),
        vmem((experts, 8, LANES), BF16), vmem((experts, 8, LANES), BF16),
        vmem((experts, 8, LANES), BF16), vmem((experts, 8, LANES), BF16),
        vmem((2, shards, feats, slots), BF16), vmem((2, units, slots), F32),
        vmem((2, CHIPS, feats, slots), F32), vmem((2, CHIPS, feats, slots), BF16), vmem((2, CHIPS, feats, slots), BF16),
        vmem((2, 3, feats, slots), BF16), vmem((2, 3, feats, slots), BF16),
        vmem((2, 3, feats, slots), BF16), vmem((2, 3, feats, slots), BF16),
        vmem((2, 2, feats // 2, slots), BF16), vmem((2, 2, feats // 2, slots), BF16),
        vmem((toks, feats), BF16), vmem((toks, feats), BF16), vmem((width, units), BF16),
        dma((8,)), dma((6,)), dma((2, 17)), dma((2, 17)), dma((2, 16)), dma((2, 16)), dma((3,)),
    ]
    return pl.pallas_call(
        functools.partial(kernel, (experts, toks, feats, units)),
        out_shape=(
            jax.ShapeDtypeStruct((toks, feats), BF16),
            jax.ShapeDtypeStruct((toks, feats), BF16),
            jax.ShapeDtypeStruct((1, width, units), BF16),
        ),
        in_specs=[pl.BlockSpec(memory_space=pl.ANY)] * 8,
        out_specs=(pl.BlockSpec(memory_space=pl.ANY),) * 3,
        scratch_shapes=scratch,
        compiler_params=pltpu.CompilerParams(
            collective_id=0, has_side_effects=True, vmem_limit_bytes=48 * 1024 * 1024
        ),
    )(tokens, routes.T, gates.T, clusters.T, counts, w_in, w_out, cotangent)


def solution(mesh):
    in_specs = (
        P("expert", None),
        P("expert", None),
        P("expert", None),
        P("expert", None),
        P("expert", None),
        P("expert", None, "dp"),
        P("expert", "dp", None),
        P("expert", None),
    )
    out_specs = (P("expert", "dp"), P("expert", "dp"), P("expert", None, "dp"))
    return jax.shard_map(
        on_device, mesh=mesh, in_specs=in_specs, out_specs=out_specs, check_vma=False
    )
```

time: 219 us -> 88.4 us (0.40)
  waiting for transfers between devices: 120 us -> 0 us
  Pallas kernels: 0 us -> 79.4 us
  starting transfers between devices: 49.4 us -> 0 us
  matrix products: 14.7 us -> 0 us
  between operations: 14.2 us -> 0.71 us
  local copies, waits for them, and re-layouts: 16 us -> 8.12 us
  other arithmetic: 3.97 us -> 0 us
    pallas_call x0 -> x1, Pallas kernels: none -> 79.4 us  [on_device(): pl.pallas_call(functools.partial(kernel, (experts, toks, feats, units)),...]
    all_to_all x4 -> x0, waiting for transfers between devices: 62.1 us -> none  [the longest x1 21.9 us: on_device(): lax.all_to_all(centre.reshape(experts, SLOTS, feature_total), 'expert', s...]
    unnamed x2 -> x0, waiting for transfers between devices: 57.7 us -> none
    all_to_all x4 -> x0, starting transfers between devices: 49.4 us -> none  [the longest x1 23.3 us: on_device(): lax.all_to_all(centre.reshape(experts, SLOTS, feature_total), 'expert', s...]
    dot_general x9 -> x0, matrix products: 14.7 us -> none  [the longest x1 3.52 us: on_device(): lax.dot_general(weighted, cotangent.astype(jnp.float32), (((0,), (0,)), (...]
    reshape x4 -> x0, local copies, waits for them, and re-layouts: 8.29 us -> none  [the longest x1 3.19 us: on_device(): back_rows = back_recv.reshape(-1, feature_total)]
    unnamed x15 -> x17, local copies, waits for them, and re-layouts: 5.41 us -> 6.61 us
  transfers between devices with their start and end apart: 5 -> 0, of which waited for: 5 -> 0; matrix products, arithmetic and copies ran while one was open for 6% -> 0% of each run, Pallas kernels for 0% -> 0%
where the time goes in v1:
time: 88.4 us; the launch traced here: 88.2 us
  Pallas kernels  79.4 us (90%)
  local copies, waits for them, and re-layouts  8.12 us (9%)
    pallas_call x1, Pallas kernels, on_device(): pl.pallas_call(functools.partial(kernel, (experts, toks, feats, units)),...  79.4 us
    unnamed x17, local copies, waits for them, and re-layouts  6.61 us

profile of v1, /device:TPU:16, one launch (start us, length us, event | category | flops | bytes accessed | tf_op | source)
XLA Modules:
  0.0 88.2 jit_solution(4862219883189602972)
XLA Ops:
  0.6 0.0 copy-start
  0.6 0.0 copy-start.3
  0.7 0.0 copy-start.4
  0.7 0.0 copy-start.5
  0.7 0.0 copy-start.6
  0.7 2.7 %copy.11.w_in = bf16[1,3584,152]{2,1,0:T(8,128)(2,1)} copy(bf16[1,3584,152]{1,2,0:T(8,128)(2,1)} %param.13) | data formatting | bytes 2179072 | tf_op args[5]
  3.4 0.0 copy-done
  3.4 0.0 copy-done.3
  3.4 0.0 copy-done.4
  3.4 0.0 copy-done.5
  3.4 0.0 copy-done.6
  3.5 0.0 copy-start.1
  3.5 1.3 %copy-done.1 = bf16[192,3584]{1,0:T(8,128)(2,1)S(1)} copy-done((bf16[192,3584]{1,0:T(8,128)(2,1)S(1)}, bf16[192,3584]{1,0:T(8,128)(2,1)}, u32[]{:S(2)}) %copy-start.1) | copy-done | bytes 1376280
  4.8 0.0 copy-start.2
  4.8 1.2 %copy-done.2 = bf16[1,152,3584]{2,1,0:T(8,128)(2,1)S(1)} copy-done((bf16[1,152,3584]{2,1,0:T(8,128)(2,1)S(1)}, bf16[1,152,3584]{2,1,0:T(8,128)(2,1)}, u32[]{:S(2)}) %copy-start.2) | copy-done | bytes 1089560
  6.0 79.4 %shard_map.103 = (bf16[192,224]{1,0:T(8,128)(2,1)S(1)}, bf16[192,224]{1,0:T(8,128)(2,1)S(1)}, bf16[1,3584,152]{2,1,0:T(8,128)(2,1)S(1)}) custom-call(bf16[192,3584]{1,0:T(8,128)(2,1)S(1)} %copy-done, s32[2,192]{1,0:T(2,128)S(1)} %bitcast.3, f32[2,192]{1,0:T(2,128)S(1)} %bitcast.4, s32[2,192]{1,0:T(2,128)S(1)} %bitcast.5, s32[1,64]{1,0:T(1,128)S(1)} %copy-done.6, ...), custom_call_target="tpu_custom_call" | custom-call | tf_op jit(solution)/shard_map/pallas_call | solution.py:399
  85.4 1.5 %copy.12 = bf16[1,3584,152]{1,2,0:T(8,128)(2,1)} copy(bf16[1,3584,152]{2,1,0:T(8,128)(2,1)S(1)} %get-tuple-element.5) | data formatting | bytes 2179072 | tf_op jit(solution)/shard_map/pallas_call | solution.py:399
  86.9 0.6 copy.15
  87.5 0.6 copy.16
Async XLA Ops:
  0.6 2.8 %copy-start = (bf16[192,3584]{1,0:T(8,128)(2,1)S(1)}, bf16[192,3584]{1,0:T(8,128)(2,1)}, u32[]{:S(2)}) copy-start(bf16[192,3584]{1,0:T(8,128)(2,1)} %tokens.1) | copy-start | bytes 4128772
  0.6 2.8 %copy-start.3 = (s32[192,2]{0,1:T(2,128)S(1)}, s32[192,2]{0,1:T(2,128)}, u32[]{:S(2)}) copy-start(s32[192,2]{0,1:T(2,128)} %param.9) | copy-start | bytes 4612
  0.7 2.8 %copy-start.4 = (f32[192,2]{0,1:T(2,128)S(1)}, f32[192,2]{0,1:T(2,128)}, u32[]{:S(2)}) copy-start(f32[192,2]{0,1:T(2,128)} %param.10) | copy-start | bytes 4612
  0.7 2.8 %copy-start.5 = (s32[192,2]{0,1:T(2,128)S(1)}, s32[192,2]{0,1:T(2,128)}, u32[]{:S(2)}) copy-start(s32[192,2]{0,1:T(2,128)} %param.11) | copy-start | bytes 4612
  0.7 2.8 %copy-start.6 = (s32[1,64]{1,0:T(1,128)S(1)}, s32[1,64]{1,0:T(1,128)}, u32[]{:S(2)}) copy-start(s32[1,64]{1,0:T(1,128)} %counts.1) | copy-start | bytes 772
  3.5 1.3 %copy-start.1 = (bf16[192,3584]{1,0:T(8,128)(2,1)S(1)}, bf16[192,3584]{1,0:T(8,128)(2,1)}, u32[]{:S(2)}) copy-start(bf16[192,3584]{1,0:T(8,128)(2,1)} %cotangent.1) | copy-start | bytes 4128772
  4.8 1.2 %copy-start.2 = (bf16[1,152,3584]{2,1,0:T(8,128)(2,1)S(1)}, bf16[1,152,3584]{2,1,0:T(8,128)(2,1)}, u32[]{:S(2)}) copy-start(bf16[1,152,3584]{2,1,0:T(8,128)(2,1)} %w_out.1) | copy-start | bytes 3268612

commit v2 on v1

v2 whole, which is shorter than its diff:
```python
import functools

import jax
import jax.numpy as jnp
from jax import lax
from jax.experimental import pallas as pl
from jax.experimental.pallas import tpu as pltpu
from jax.sharding import PartitionSpec as P

SLOTS = 2
LANES = 128
CHIPS = 8
MESH = pl.DeviceIdType.MESH
BF16 = jnp.bfloat16
F32 = jnp.float32

def nn(a, b):
    return lax.dot_general(a, b, (((1,), (0,)), ((), ())), preferred_element_type=F32)


def nt(a, b):
    return lax.dot_general(a, b, (((1,), (1,)), ((), ())), preferred_element_type=F32)


def split(value):
    high = value.astype(BF16)
    return high, (value - high.astype(F32)).astype(BF16)


def eye(size):
    rows = lax.broadcasted_iota(jnp.int32, (size, size), 0)
    return (rows == lax.broadcasted_iota(jnp.int32, (size, size), 1)).astype(BF16)


def kernel(
    shape,
    tokens, routes, gates, clusters, counts, w_in, w_out, cotangent,
    mixed_out, grad_tokens_out, grad_w_out,
    tok_win, cot_win, routes_v, gates_v, clusters_v, counts_v, win_v, wout_v,
    tok_q, cot_q, win_r, wout_r, perm, perm_t,
    either_t, weight_t, either_r, weight_r, gate_col, member_v, tok_s, cot_s, centre_v, back_v,
    send1, recv1, send2, recv2,
    gathered, pre_v, part, sib_out, sib_in, right_out, left_out, right_in, left_in,
    in_sem, hop_sem, ag_send, ag_recv, rs_send, rs_recv,
):
    experts, toks, feats, units = shape
    slots = experts * SLOTS
    half = feats // 2
    halves = ((0, half), (half, half))
    upper = feats - LANES
    dp = lax.axis_index("dp")
    me = lax.axis_index("expert")
    chip = dp // 2
    core = lax.rem(dp, 2)
    right = lax.rem(chip + 1, CHIPS) * 2 + core
    left = lax.rem(chip + CHIPS - 1, CHIPS) * 2 + core
    right_2 = lax.rem(chip + 2, CHIPS) * 2 + core
    left_2 = lax.rem(chip + CHIPS - 2, CHIPS) * 2 + core
    sibling = chip * 2 + 1 - core

    def far_first(i):
        if experts != CHIPS * CHIPS:
            return lax.rem(me + i + 1, experts)

        def away(j):
            return 4 + (j + 1) // 2 * (1 - 2 * (j % 2))

        row = lax.rem(me // CHIPS + away(i // CHIPS), CHIPS)
        column = lax.rem(lax.rem(me, CHIPS) + away(i % CHIPS), CHIPS)
        return row * CHIPS + column

    def shard(distance, of_core):
        return lax.rem(chip + distance, CHIPS) * 2 + of_core

    width = tokens.shape[1]
    window = tok_win.shape[1]
    tile = jnp.minimum(dp * feats // LANES, (width - window) // LANES)
    start = pl.multiple_of(tile * LANES, LANES)
    shift = dp * feats - tile * LANES
    quarter = width // 4
    parity = lax.rem(chip, 2)
    mine, near = 2 * parity + core, 2 * (1 - parity) + core
    own_quarter = pl.ds(pl.multiple_of(mine * quarter, LANES), quarter)

    loads = [
        pltpu.make_async_copy(src, dst, in_sem.at[i])
        for i, (src, dst) in enumerate((
            (routes, routes_v), (clusters, clusters_v), (gates, gates_v), (counts, counts_v),
            (tokens.at[:, own_quarter], tok_q),
            (cotangent.at[:, own_quarter], cot_q),
            (tokens.at[:, pl.ds(start, window)], tok_win),
            (cotangent.at[:, pl.ds(start, window)], cot_win),
            (w_out.at[0], wout_v), (w_in.at[0], win_v),
        ))
    ]
    for load in loads[:6]:
        load.start()

    barrier = pltpu.get_barrier_semaphore()

    @pl.loop(0, experts - 1)
    def _(i):
        pl.semaphore_signal(barrier, inc=1, device_id=(dp, far_first(i)), device_id_type=MESH)

    for there in (right, left, right_2, left_2, sibling):
        pl.semaphore_signal(barrier, inc=1, device_id=(there, me), device_id_type=MESH)

    for load in loads[6:]:
        load.start()

    rows = lax.broadcasted_iota(jnp.int32, (4 * slots, 4 * slots), 0)
    cols = lax.broadcasted_iota(jnp.int32, (4 * slots, 4 * slots), 1)
    perm[...] = (cols == ((rows % 8) // 2) * slots + (rows // 8) * 2 + rows % 2).astype(F32).astype(BF16)

    for load in loads[:4]:
        load.wait()
    expert_rows = lax.broadcasted_iota(jnp.int32, (experts, experts), 0)
    expert_cols = lax.broadcasted_iota(jnp.int32, (experts, experts), 1)
    live_col = jnp.sum(jnp.where(expert_rows == expert_cols, counts_v[...], 0), axis=1, keepdims=True)
    ids = lax.broadcasted_iota(jnp.int32, (experts, toks), 0)
    slot_rows = lax.broadcasted_iota(jnp.int32, (slots, toks), 0)
    hits, weights = [], []
    for k in range(2):
        route = routes_v[k : k + 1, :]
        live = jnp.sum(jnp.where(ids == route, live_col, 0), axis=0, keepdims=True)
        slot = route * SLOTS + jnp.where(live == 2, clusters_v[k : k + 1, :] & 1, 0)
        hits.append((slot_rows == slot).astype(F32))
        weights.append(hits[-1] * gates_v[k : k + 1, :])
    either = hits[0] + hits[1]
    weight_hi, weight_lo = split(weights[0] + weights[1])
    member = jnp.maximum(jnp.sum(either, axis=1, keepdims=True), 1.0)
    member_v[...] = jnp.broadcast_to(member, member_v.shape)
    either_t[...] = either.astype(BF16)
    weight_t[0] = weight_hi
    weight_t[1] = weight_lo

    def exchange(send, recv, sem):
        own = pltpu.make_async_copy(send.at[me], recv.at[me], hop_sem.at[sem])
        own.start()

        @pl.loop(0, experts - 1)
        def _(i):
            peer = far_first(i)
            pltpu.make_async_remote_copy(
                src_ref=send.at[peer], dst_ref=recv.at[me],
                send_sem=hop_sem.at[sem + 1], recv_sem=hop_sem.at[sem + 2],
                device_id=(dp, peer), device_id_type=MESH,
            ).start()

        return own

    def exchanged(own, send, recv, sem):
        own.wait()
        rest = pl.ds(0, experts - 1)
        pltpu.make_async_copy(recv.at[rest], recv.at[rest], hop_sem.at[sem + 2]).wait()

    def sent_all(send, sem):
        rest = pl.ds(0, experts - 1)
        pltpu.make_async_copy(send.at[rest], send.at[rest], hop_sem.at[sem + 1]).wait()

    def spread(rows_of):
        last = jnp.concatenate([rows_of[:, 6 * LANES :], jnp.zeros((slots, LANES), BF16)], axis=1)
        stacked = jnp.concatenate([rows_of[:, 2 * i * LANES : 2 * (i + 1) * LANES] for i in range(3)] + [last], axis=0)
        return nn(perm[...], stacked).astype(BF16).reshape(experts, 8, 2 * LANES)

    loads[4].wait()
    send1[0] = spread((nn(either_t[...], tok_q[...]) / member).astype(BF16))
    pl.semaphore_wait(barrier, experts + 4)
    owns = [exchange(send1.at[0], recv1.at[0], 0)]
    loads[5].wait()
    send1[1] = spread((nn(weight_t[0], cot_q[...]) + nn(weight_t[1], cot_q[...])).astype(BF16))
    owns.append(exchange(send1.at[1], recv1.at[1], 3))

    pick_rows = lax.broadcasted_iota(jnp.int32, (window, 2 * LANES), 0)
    pick_cols = lax.broadcasted_iota(jnp.int32, (window, 2 * LANES), 1)
    pick = ((pick_rows == pick_cols + shift) & (pick_cols < feats)).astype(F32).astype(BF16)
    loads[6].wait()
    tok_s[...] = nn(tok_win[...], pick).astype(BF16)
    centre_v[...] = (nn(either_t[...], tok_s[...]) / member_v[...]).astype(BF16)
    loads[7].wait()
    cot_s[...] = nn(cot_win[...], pick).astype(BF16)
    back_v[...] = nn(weight_t[0], cot_s[...]) + nn(weight_t[1], cot_s[...])
    perm_t[...] = (rows == ((cols % 8) // 2) * slots + (cols // 8) * 2 + cols % 2).astype(F32).astype(BF16)
    token_eye = eye(toks)
    either_r[...] = nt(token_eye, either_t[...]).astype(BF16)
    weight_r[0] = nt(token_eye, weight_t[0]).astype(BF16)
    weight_r[1] = nt(token_eye, weight_t[1]).astype(BF16)
    gate_row = 1.0 + jnp.sum(gates_v[...], axis=0, keepdims=True)
    gate_col[...] = jnp.broadcast_to(
        jnp.sum(jnp.where(token_eye.astype(F32) > 0.0, gate_row, 0.0), axis=1, keepdims=True), gate_col.shape
    )
    loads[8].wait()
    loads[9].wait()
    lane_eye = eye(2 * LANES)

    @pl.loop(0, width // (2 * LANES))
    def _(j):
        at = pl.ds(pl.multiple_of(j * 2 * LANES, LANES), 2 * LANES)
        win_r[at, :] = nt(lane_eye, win_v[:, at]).astype(BF16)
        wout_r[at, :] = nt(lane_eye, wout_v[:, at]).astype(BF16)

    pending = []

    def pass_on(kind, lane, which, rows, there):
        at = pl.ds(*rows)
        copy = pltpu.make_async_remote_copy(
            src_ref=gathered.at[kind, which, at], dst_ref=gathered.at[kind, which, at],
            send_sem=ag_send.at[kind, lane], recv_sem=ag_recv.at[kind, lane],
            device_id=(there, me), device_id_type=MESH,
        )
        copy.start()
        pending.append(copy)

    def landed(kind, lane, which, rows):
        here = gathered.at[kind, which, pl.ds(*rows)]
        pltpu.make_async_copy(here, here, ag_recv.at[kind, lane]).wait()

    whole, first, second = (0, quarter), (0, quarter // 2), (quarter // 2, quarter // 2)
    projections = (win_v, wout_v)

    def contract(kind, which):
        columns = pl.ds(pl.multiple_of(which * quarter, LANES), quarter)
        return nn(projections[kind][:, columns], gathered[kind, which])

    def arrive(kind):
        exchanged(owns[kind], send1.at[kind], recv1.at[kind], 3 * kind)
        arrived = lax.dot_general(
            recv1[kind].reshape(4 * slots, 2 * LANES), perm[...], (((0,), (0,)), ((), ())), preferred_element_type=F32
        ).astype(BF16)
        for i in range(4):
            count = 2 * LANES if i < 3 else LANES
            low = 2 * i * LANES
            gathered[kind, mine, low : low + count, :] = arrived[:count, i * slots : (i + 1) * slots]
        pass_on(kind, 0, mine, first, right)
        pass_on(kind, 1, mine, second, left)
        pass_on(kind, 2, mine, whole, sibling)
        pre_v[kind] = contract(kind, mine)

    def relay(kind):
        landed(kind, 0, near, first)
        pass_on(kind, 3, near, first, sibling)
        landed(kind, 1, near, second)
        pass_on(kind, 4, near, second, sibling)

    def complete(kind):
        others = 2 * parity + 1 - core, 2 * (1 - parity) + 1 - core
        total = pre_v[kind] + contract(kind, near)
        landed(kind, 2, others[0], whole)
        total += contract(kind, others[0])
        landed(kind, 3, others[1], first)
        landed(kind, 4, others[1], second)
        return total + contract(kind, others[1])

    summed = []
    def push(kind, lane, out, into, there):
        copy = pltpu.make_async_remote_copy(
            src_ref=out, dst_ref=into,
            send_sem=rs_send.at[kind, lane], recv_sem=rs_recv.at[kind, lane],
            device_id=(there, me), device_id_type=MESH,
        )
        copy.start()
        summed.append(copy)

    def partial_sums(kind, weights_of, units_of, distances):
        for d in distances:
            theirs = pl.ds(pl.multiple_of(shard(d, 1 - core) * feats, 32), feats)
            sib_out[kind, d] = nn(weights_of[theirs, :], units_of).astype(BF16)
            push(kind, d, sib_out.at[kind, d], sib_in.at[kind, d], sibling)
            ours = pl.ds(pl.multiple_of(shard(d, core) * feats, 32), feats)
            part[kind, d] = nn(weights_of[ours, :], units_of)

    def pair(kind, d):
        pltpu.make_async_copy(sib_in.at[kind, d], sib_in.at[kind, d], rs_recv.at[kind, d]).wait()
        return part[kind, d] + sib_in[kind, d].astype(F32)

    def came(kind, lane, into):
        pltpu.make_async_copy(into, into, rs_recv.at[kind, lane]).wait()
        return into[...].astype(F32)

    lower, higher = pl.ds(*halves[0]), pl.ds(*halves[1])

    def push_far(kind):
        total = pair(kind, 4).astype(BF16)
        right_out[kind, 0, lower] = total[:half]
        push(kind, 8, right_out.at[kind, 0, lower], right_in.at[kind, 0, lower], right_2)
        left_out[kind, 0, higher] = total[half:]
        push(kind, 12, left_out.at[kind, 0, higher], left_in.at[kind, 0, higher], left_2)
        right_out[kind, 1] = pair(kind, 3).astype(BF16)
        push(kind, 9, right_out.at[kind, 1], right_in.at[kind, 1], right)
        left_out[kind, 1] = pair(kind, 5).astype(BF16)
        push(kind, 13, left_out.at[kind, 1], left_in.at[kind, 1], left)

    def push_near(kind):
        right_out[kind, 2] = pair(kind, 1).astype(BF16)
        push(kind, 10, right_out.at[kind, 2], right_in.at[kind, 2], right)
        left_out[kind, 2] = pair(kind, 7).astype(BF16)
        push(kind, 14, left_out.at[kind, 2], left_in.at[kind, 2], left)
        part[kind, 2] = pair(kind, 2)
        part[kind, 6] = pair(kind, 6)
        part[kind, 0] = pair(kind, 0)

    def push_joined(kind):
        total = part[kind, 2] + came(kind, 9, right_in.at[kind, 1])
        right_out[kind, 3, higher] = total[half:].astype(BF16)
        right_out[kind, 3, lower] = (total[:half] + came(kind, 8, right_in.at[kind, 0, lower])).astype(BF16)
        push(kind, 11, right_out.at[kind, 3], right_in.at[kind, 3], right_2)
        total = part[kind, 6] + came(kind, 13, left_in.at[kind, 1])
        left_out[kind, 3, lower] = total[:half].astype(BF16)
        left_out[kind, 3, higher] = (total[half:] + came(kind, 12, left_in.at[kind, 0, higher])).astype(BF16)
        push(kind, 15, left_out.at[kind, 3], left_in.at[kind, 3], left_2)

    def summed_up(kind):
        total = part[kind, 0] + came(kind, 10, right_in.at[kind, 2]) + came(kind, 14, left_in.at[kind, 2])
        total += came(kind, 11, right_in.at[kind, 3]) + came(kind, 15, left_in.at[kind, 3])
        return total.astype(BF16)

    def weight_grads(group):
        grad_w_out[0, :, group * quarter : (group + 1) * quarter] = nt(preact_grad, gathered[0, group]).astype(BF16)

    arrive(0)
    arrive(1)
    relay(0)
    preact = complete(0)
    sigmoid_val = jax.nn.sigmoid(preact)
    hidden = (preact * sigmoid_val).astype(BF16)
    slope = sigmoid_val * (1.0 + preact * (1.0 - sigmoid_val))
    partial_sums(0, wout_r, hidden, (4, 3, 5))
    push_far(0)
    partial_sums(0, wout_r, hidden, (1, 7, 2, 6, 0))
    push_near(0)
    relay(1)
    preact_grad = (complete(1) * slope).astype(BF16)
    partial_sums(1, win_r, preact_grad, (4, 3, 5))
    push_joined(0)
    push_far(1)
    partial_sums(1, win_r, preact_grad, (1, 7, 2, 6, 0))
    push_near(1)
    weight_grads(0)
    weight_grads(1)
    push_joined(1)
    weight_grads(2)
    weight_grads(3)

    pieces = []
    for kind in range(2):
        total = summed_up(kind)
        pieces += [total[:LANES], jnp.concatenate([total[LANES:], jnp.zeros((LANES - upper, slots), BF16)], axis=0)]
    send2[...] = nt(perm[...], jnp.concatenate(pieces, axis=1)).astype(BF16).reshape(experts, 8, LANES)
    own2 = exchange(send2, recv2, 6)

    scaled_tok = [tok_s[:, i * LANES : (i + 1) * LANES].astype(F32) * gate_col[...] for i in range(2)]
    scaled_cot = [cot_s[:, i * LANES : (i + 1) * LANES].astype(F32) * gate_col[...] for i in range(2)]
    scale = 1.0 / member_v[:, :LANES]
    for copy in pending + summed:
        copy.wait_send()
    sent_all(send1.at[0], 0)
    sent_all(send1.at[1], 3)

    exchanged(own2, send2, recv2, 6)
    ordered = nn(perm_t[...], recv2[...].reshape(4 * slots, LANES))
    for i, (low, count) in enumerate(((0, LANES), (LANES, upper))):
        carried = ordered[i * slots : (i + 1) * slots] - centre_v[:, i * LANES : (i + 1) * LANES].astype(F32)
        pulled = (ordered[(2 + i) * slots : (3 + i) * slots] - back_v[:, i * LANES : (i + 1) * LANES]) * scale
        high, rest = split(carried)
        mixed = scaled_tok[i] + nn(weight_r[0], high) + nn(weight_r[0], rest) + nn(weight_r[1], high)
        mixed_out[:, low : low + count] = mixed[:, :count].astype(BF16)
        high, rest = split(pulled)
        grads = scaled_cot[i] + nn(either_r[...], high) + nn(either_r[...], rest)
        grad_tokens_out[:, low : low + count] = grads[:, :count].astype(BF16)
    sent_all(send2, 6)


def on_device(tokens, routes, gates, clusters, counts, w_in, w_out, cotangent):
    toks, width = tokens.shape
    experts = counts.shape[1]
    shards = lax.axis_size("dp")
    units = w_in.shape[2]
    feats = width // shards
    slots = experts * SLOTS
    vmem = pltpu.VMEM
    dma = pltpu.SemaphoreType.DMA
    scratch = [
        vmem((toks, 3 * LANES), BF16), vmem((toks, 3 * LANES), BF16),
        vmem((2, toks), jnp.int32), vmem((2, toks), F32), vmem((2, toks), jnp.int32), vmem((1, experts), jnp.int32),
        vmem((units, width), BF16), vmem((units, width), BF16),
        vmem((toks, width // 4), BF16), vmem((toks, width // 4), BF16),
        vmem((width, units), BF16), vmem((width, units), BF16),
        vmem((4 * slots, 4 * slots), BF16), vmem((4 * slots, 4 * slots), BF16),
        vmem((slots, toks), BF16), vmem((2, slots, toks), BF16),
        vmem((toks, slots), BF16), vmem((2, toks, slots), BF16),
        vmem((toks, LANES), F32), vmem((slots, 2 * LANES), F32),
        vmem((toks, 2 * LANES), BF16), vmem((toks, 2 * LANES), BF16),
        vmem((slots, 2 * LANES), BF16), vmem((slots, 2 * LANES), F32),
        vmem((2, experts, 8, 2 * LANES), BF16), vmem((2, experts, 8, 2 * LANES), BF16),
        vmem((experts, 8, LANES), BF16), vmem((experts, 8, LANES), BF16),
        vmem((2, 4, width // 4, slots), BF16), vmem((2, units, slots), F32),
        vmem((2, CHIPS, feats, slots), F32), vmem((2, CHIPS, feats, slots), BF16), vmem((2, CHIPS, feats, slots), BF16),
        vmem((2, 4, feats, slots), BF16), vmem((2, 4, feats, slots), BF16),
        vmem((2, 4, feats, slots), BF16), vmem((2, 4, feats, slots), BF16),
        dma((10,)), dma((9,)), dma((2, 5)), dma((2, 5)), dma((2, 16)), dma((2, 16)),
    ]
    operands = (tokens, routes.T, gates.T, clusters.T, counts, jnp.swapaxes(w_in, 1, 2), w_out, cotangent)
    operands = [pltpu.with_memory_space_constraint(operand, pltpu.HBM) for operand in operands]
    hbm = pl.BlockSpec(memory_space=pltpu.HBM)
    mixed, grad_tokens, grad_w = pl.pallas_call(
        functools.partial(kernel, (experts, toks, feats, units)),
        out_shape=(
            jax.ShapeDtypeStruct((toks, feats), BF16),
            jax.ShapeDtypeStruct((toks, feats), BF16),
            jax.ShapeDtypeStruct((1, units, width), BF16),
        ),
        in_specs=[hbm] * 8,
        out_specs=(pl.BlockSpec(memory_space=pltpu.VMEM),) * 3,
        scratch_shapes=scratch,
        compiler_params=pltpu.CompilerParams(
            collective_id=0, has_side_effects=True, vmem_limit_bytes=48 * 1024 * 1024
        ),
    )(*operands)
    return mixed, grad_tokens, jnp.swapaxes(grad_w, 1, 2)


def solution(mesh):
    in_specs = (
        P("expert", None),
        P("expert", None),
        P("expert", None),
        P("expert", None),
        P("expert", None),
        P("expert", None, "dp"),
        P("expert", "dp", None),
        P("expert", None),
    )
    out_specs = (P("expert", "dp"), P("expert", "dp"), P("expert", None, "dp"))
    return jax.shard_map(
        on_device, mesh=mesh, in_specs=in_specs, out_specs=out_specs, check_vma=False
    )
```

time: 88.4 us -> 75.1 us (0.85)
  the two profiles are of different devices: /device:TPU:16 before, /device:TPU:4 now
where the time goes in v2:
time: 75.1 us; the launch traced here: 75 us
  Pallas kernels  72.1 us (96%)
  local copies, waits for them, and re-layouts  2.27 us (3%)
    pallas_call x1, Pallas kernels, on_device(): pl.pallas_call(functools.partial(kernel, (experts, toks, feats, units)),...  72.1 us
    unnamed x3, local copies, waits for them, and re-layouts  2.27 us

profile of v2, /device:TPU:4, one launch (start us, length us, event | category | flops | bytes accessed | tf_op | source)
XLA Modules:
  0.0 75.0 jit_solution(7979363416830950487)
XLA Ops:
  0.6 72.1 %shard_map.103 = (bf16[192,224]{1,0:T(8,128)(2,1)S(1)}, bf16[192,224]{1,0:T(8,128)(2,1)S(1)}, bf16[1,152,3584]{2,1,0:T(8,128)(2,1)S(1)}) custom-call(bf16[192,3584]{1,0:T(8,128)(2,1)} %tokens.1, s32[2,192]{1,0:T(2,128)} %bitcast.7, f32[2,192]{1,0:T(2,128)} %bitcast.8, s32[2,192]{1,0:T(2,128)} %bitcast.9, s32[1,64]{1,0:T(1,128)} %counts.1, ...), custom_call_target="tpu_custom_call" | custom-call | tf_op jit(solution)/shard_map/pallas_call | solution.py:405
  72.7 0.6 copy.14
  73.4 0.6 copy.15
  74.0 1.0 %copy.16 = bf16[1,3584,152]{1,2,0:T(8,128)(2,1)} copy(bf16[1,3584,152]{1,2,0:T(8,128)(2,1)S(1)} %bitcast.5) | data formatting | bytes 2179072

commit v3 on v2

--- a/solution.py
+++ b/solution.py
@@ -35,7 +35,7 @@
 def kernel(
     shape,
     tokens, routes, gates, clusters, counts, w_in, w_out, cotangent,
-    mixed_out, grad_tokens_out, grad_w_out,
+    tokens_out, grad_w_out,
     tok_win, cot_win, routes_v, gates_v, clusters_v, counts_v, win_v, wout_v,
     tok_q, cot_q, win_r, wout_r, perm, perm_t,
     either_t, weight_t, either_r, weight_r, gate_col, member_v, tok_s, cot_s, centre_v, back_v,
@@ -363,10 +363,10 @@
         pulled = (ordered[(2 + i) * slots : (3 + i) * slots] - back_v[:, i * LANES : (i + 1) * LANES]) * scale
         high, rest = split(carried)
         mixed = scaled_tok[i] + nn(weight_r[0], high) + nn(weight_r[0], rest) + nn(weight_r[1], high)
-        mixed_out[:, low : low + count] = mixed[:, :count].astype(BF16)
+        tokens_out[0, :, low : low + count] = mixed[:, :count].astype(BF16)
         high, rest = split(pulled)
         grads = scaled_cot[i] + nn(either_r[...], high) + nn(either_r[...], rest)
-        grad_tokens_out[:, low : low + count] = grads[:, :count].astype(BF16)
+        tokens_out[1, :, low : low + count] = grads[:, :count].astype(BF16)
     sent_all(send2, 6)
 
 
@@ -402,21 +402,20 @@
     operands = (tokens, routes.T, gates.T, clusters.T, counts, jnp.swapaxes(w_in, 1, 2), w_out, cotangent)
     operands = [pltpu.with_memory_space_constraint(operand, pltpu.HBM) for operand in operands]
     hbm = pl.BlockSpec(memory_space=pltpu.HBM)
-    mixed, grad_tokens, grad_w = pl.pallas_call(
+    token_results, grad_w = pl.pallas_call(
         functools.partial(kernel, (experts, toks, feats, units)),
         out_shape=(
-            jax.ShapeDtypeStruct((toks, feats), BF16),
-            jax.ShapeDtypeStruct((toks, feats), BF16),
+            jax.ShapeDtypeStruct((2, toks, feats), BF16),
             jax.ShapeDtypeStruct((1, units, width), BF16),
         ),
         in_specs=[hbm] * 8,
-        out_specs=(pl.BlockSpec(memory_space=pltpu.VMEM),) * 3,
+        out_specs=(pl.BlockSpec(memory_space=pltpu.VMEM),) * 2,
         scratch_shapes=scratch,
         compiler_params=pltpu.CompilerParams(
             collective_id=0, has_side_effects=True, vmem_limit_bytes=48 * 1024 * 1024
         ),
     )(*operands)
-    return mixed, grad_tokens, jnp.swapaxes(grad_w, 1, 2)
+    return token_results[0], token_results[1], jnp.swapaxes(grad_w, 1, 2)
 
 
 def solution(mesh):

time: 75.1 us -> 74.6 us (level)
  the two profiles are of different devices: /device:TPU:4 before, /device:TPU:2 now
where the time goes in v3:
time: 74.6 us; the launch traced here: 74.5 us
  Pallas kernels  72.1 us (97%)
  local copies, waits for them, and re-layouts  1.67 us (2%)
    pallas_call x1, Pallas kernels, on_device(): pl.pallas_call(functools.partial(kernel, (experts, toks, feats, units)),...  72.1 us

profile of v3, /device:TPU:2, one launch (start us, length us, event | category | flops | bytes accessed | tf_op | source)
XLA Modules:
  0.0 74.5 jit_solution(305026484193760990)
XLA Ops:
  0.6 72.1 %shard_map.103 = (bf16[2,192,224]{2,1,0:T(8,128)(2,1)S(1)}, bf16[1,152,3584]{2,1,0:T(8,128)(2,1)S(1)}) custom-call(bf16[192,3584]{1,0:T(8,128)(2,1)} %tokens.1, s32[2,192]{1,0:T(2,128)} %bitcast.11, f32[2,192]{1,0:T(2,128)} %bitcast.12, s32[2,192]{1,0:T(2,128)} %bitcast.13, s32[1,64]{1,0:T(1,128)} %counts.1, bf16[1,152,3584]{2,1,0:T(8,128)(2,1)} %bitcast.10, ...), custom_call_target="tpu_custom_call" | custom-call | tf_op jit(solution)/shard_map/pallas_call | solution.py:405
  72.8 0.7 slice_bitcast_fusion
  73.5 1.0 %copy.12 = bf16[1,3584,152]{1,2,0:T(8,128)(2,1)} copy(bf16[1,3584,152]{1,2,0:T(8,128)(2,1)S(1)} %bitcast.9) | data formatting | bytes 2179072
